TPU v7x, 32 devices: a whole 2x2x4 slice. The times are simulated.
32 devices in a mesh: row: 4 (over y, x), col: 8 (over z, core).
Axes of the slice: x: 2, y: 2, z: 4, core: 2. Of those that a mesh axis runs over, the one named last changes fastest.
Arguments:
- front: float32 [16, 1024, 8, 2048], P(None, 'row', None, 'col'), may hold values from -6 to 6
- children: float32 [8, 4096, 4096], P('row', None, 'col'), may hold values from -6 to 6
- child_rows: int32 [8, 16], replicated, may hold values from 0 to 63, as said below
- owner_slots: int32 [8], replicated, may hold values from 0 to 1, as said below
- inverses: float32 [3, 256, 256], replicated, may hold values from -0.0390625 to 0.0390625
- pattern: int32 [64, 64], replicated, may hold values 0 or 1
Outputs:
- factored: float32 [16, 1024, 8, 2048], P(None, 'row', None, 'col')
Inputs may be any that keep to these rules, and one draw needn't show every extreme that they name: `child_rows`: the 16 entries of one slot are distinct. For each slot g there is an offset o_g such that entry k taken mod 8 equals (k // (16 / 8) + o_g) mod 8, and every offset 0 to 8 - 1 belongs to exactly 8 / 8 slots. Hence each residue mod 4 appears exactly 16 / 4 times in each slot. `owner_slots`: slots g = o * 2 + s belong to owner o; an owner's live slots come first, slot 0 of every owner is live, at least one owner has all 2 slots live and at least one other owner has fewer.
All inputs are finite; a program needn't handle non-finite values.
Results may differ from a plain program's by a relative error of at most 0.00014.
Values sent between devices are 32-bit elements; how exact they have to be, the bound alone decides.
A program may use at most 320 MiB of HBM per device.

v0:
```python
import jax
import jax.numpy as jnp
from jax import lax
from jax.sharding import PartitionSpec as P

precise = lax.Precision.HIGHEST


def from_root(block, axis, holder):
    block = jnp.where(lax.axis_index(axis) == holder, block, jnp.zeros_like(block))
    return lax.psum(block, axis)


def shards(front, children, child_rows, owner_slots, inverses, pattern):
    rows_n = lax.axis_size("row")
    cols_n = lax.axis_size("col")
    my_row = lax.axis_index("row")
    my_col = lax.axis_index("col")
    local_rows, tile_size, local_cols, _ = front.shape
    slots_here, child_order, child_width = children.shape
    kblocks = child_order // tile_size
    per_row = kblocks // rows_n
    per_col = child_width // tile_size
    slot_total = child_rows.shape[0]
    per_dest = slot_total // cols_n
    panel_count = inverses.shape[0]
    col_ratio = cols_n // rows_n
    position = jnp.arange(kblocks, dtype=jnp.int32)
    row_order = jnp.argsort(child_rows % rows_n * kblocks + position[None, :], axis=1)
    my_order = lax.dynamic_slice_in_dim(row_order, my_row * slots_here, slots_here, 0)
    my_rank = lax.dynamic_slice_in_dim(row_order, my_row * per_row, per_row, 1)
    row_blocks = jnp.take_along_axis(child_rows, my_rank, axis=1)
    col_blocks = child_rows.reshape(slot_total, cols_n, per_col)
    slot_ids = jnp.arange(slot_total, dtype=jnp.int32)
    local_row_ids = jnp.arange(local_rows, dtype=jnp.int32)
    local_col_ids = jnp.arange(local_cols, dtype=jnp.int32)
    blocks_in = children.reshape(slots_here, kblocks, tile_size, child_width)
    sorted_rows = jnp.take_along_axis(blocks_in, my_order[:, :, None, None], axis=1)
    outgoing = sorted_rows.reshape(slots_here, rows_n, per_row, tile_size, child_width)
    arrived = lax.all_to_all(outgoing, "row", split_axis=1, concat_axis=0, tiled=True)
    arrived = arrived.reshape(slot_total, per_row, tile_size, child_width)
    dest_by_src = jnp.transpose(col_blocks[:, :, 0] % cols_n)
    send_order = jnp.argsort(dest_by_src * slot_total + slot_ids[None, :], axis=1)
    my_send = lax.dynamic_index_in_dim(send_order, my_col, 0, keepdims=False)
    outgoing = jnp.take(arrived, my_send, axis=0).reshape(
        cols_n, per_dest, per_row, tile_size, child_width
    )
    landed = lax.all_to_all(outgoing, "col", split_axis=0, concat_axis=0, tiled=True)
    recv_slot = lax.dynamic_slice_in_dim(send_order, my_col * per_dest, per_dest, 1)
    got_rows = row_blocks[recv_slot]
    src_ids = jnp.arange(cols_n, dtype=jnp.int32)
    got_cols = col_blocks[recv_slot, src_ids[:, None]]
    live_flag = owner_slots[recv_slot].astype(jnp.float32)
    row_hits = ((got_rows // rows_n)[..., None] == local_row_ids).astype(jnp.float32)
    row_hits = row_hits * live_flag[:, :, None, None]
    col_hits = ((got_cols // cols_n)[..., None] == local_col_ids).astype(jnp.float32)
    pieces = landed.reshape(cols_n, per_dest, per_row, tile_size, per_col, tile_size)
    extend_sum = jnp.einsum("snpa,sntb,snpxty->axby", row_hits, col_hits, pieces, precision=precise)
    summed_front = front + extend_sum
    block_index = local_row_ids * rows_n + my_row
    col_index = local_col_ids * cols_n + my_col
    top_index = my_col // rows_n
    top_root = my_col % rows_n
    current = summed_front[:, :, 0, :]
    factors = []
    for step_index in range(panel_count):
        column = from_root(current, "col", step_index)
        factor = jnp.einsum("axy,zy->axz", column, inverses[step_index], precision=precise)
        factor = jnp.where(
            (block_index >= step_index)[:, None, None], factor, jnp.zeros_like(factor)
        )
        factors.append(factor)
        if step_index + 1 < panel_count:
            top_block = lax.dynamic_index_in_dim(factor, top_index, 0, keepdims=False)
            top_block = from_root(top_block, "row", top_root)
            reduced = current - jnp.einsum("axy,zy->axz", factor, top_block, precision=precise)
            current = jnp.where(my_col > step_index, reduced, current)
    lower = jnp.concatenate(factors, axis=2)
    lower_split = lower.reshape(local_cols, col_ratio, tile_size, panel_count * tile_size)
    chosen = lax.dynamic_index_in_dim(lower_split, top_index, 1, keepdims=False)
    across = from_root(chosen, "row", top_root)
    trailing_sum = jnp.einsum("axk,byk->axby", lower, across, precision=precise)
    block_mask = pattern.reshape(local_rows, rows_n, local_cols, cols_n)
    block_mask = lax.dynamic_index_in_dim(block_mask, my_row, 1, keepdims=False)
    block_mask = lax.dynamic_index_in_dim(block_mask, my_col, 2, keepdims=False)
    trailing = (
        (block_mask > 0)
        & (block_index >= panel_count)[:, None]
        & (col_index >= panel_count)[None, :]
    )
    result = jnp.where(trailing[:, None, :, None], summed_front - trailing_sum, summed_front)
    stacked = jnp.stack(factors, axis=0)
    mine_factor = lax.dynamic_index_in_dim(
        stacked, jnp.minimum(my_col, panel_count - 1), 0, keepdims=False
    )
    first_col = jnp.where(my_col < panel_count, mine_factor, result[:, :, 0, :])
    result = result.at[:, :, 0, :].set(first_col)
    return result


def solution(mesh):
    return jax.shard_map(
        shards,
        mesh=mesh,
        in_specs=(P(None, "row", None, "col"), P("row", None, "col"), P(), P(), P(), P()),
        out_specs=P(None, "row", None, "col"),
        check_vma=False,
    )
```

profile of v0, /device:TPU:0, one launch (start us, length us, event | category | flops | bytes accessed | tf_op | source)
XLA Modules:
  0.0 1667.9 jit_solution(10317902727512108828)
XLA Ops:
  8.5 14.7 gather_fusion.4
  46.3 182.8 %all-to-all-done = f32[2,4,4,256,512]{4,3,2,0,1:T(8,128)} async-done(((f32[2,4,4,256,512]{4,3,2,0,1:T(8,128)}), f32[2,4,4,256,512]{4,3,2,0,1:T(8,128)}, u32[]{:S(2)}, u32[]{:S(2)}) %all-to-all-start) | async-done | bytes 16777248 | tf_op jit(solution)/shard_map/all_to_all | solution.py:40
  229.1 14.2 gather_fusion
  243.3 12.3 fusion.2
  265.1 360.1 %all-to-all-done.1 = f32[8,1,4,256,512]{4,3,2,1,0:T(8,128)} async-done(((f32[8,1,4,256,512]{4,3,2,1,0:T(8,128)}), f32[8,1,4,256,512]{4,3,2,1,0:T(8,128)}, u32[]{:S(2)}, u32[]{:S(2)}) %all-to-all-start.1) | async-done | bytes 16777248 | tf_op jit(solution)/shard_map/all_to_all | solution.py:48
  625.2 17.4 %copy.158 = f32[8,1,4,256,512]{3,4,2,0,1:T(8,128)} copy(f32[8,1,4,256,512]{4,3,2,1,0:T(8,128)} %all-to-all-done.1) | data formatting | bytes 33554432 | tf_op jit(solution)/shard_map/all_to_all | solution.py:48
  642.5 19.8 %copy.162 = f32[8,4,256,2,256]{4,1,3,2,0:T(4,128)} copy(f32[8,4,256,2,256]{2,4,3,1,0:T(8,128)} %bitcast.125) | data formatting | bytes 33554432 | tf_op jit(solution)/shard_map/reshape.50
  662.4 59.5 %fusion.20 = f32[8,256,2,256,16]{3,4,2,1,0:T(8,128)} fusion(f32[8,4,256,2,256]{4,1,3,2,0:T(4,128)} %copy.162, f32[8]{0:T(128)S(1)} %convert_element_type.16, s32[8,4]{1,0:T(8,128)S(1)} %add_select_fusion.2), kind=kOutput, calls=%fused_computation.46 | convolution fusion | flops 805307392 | bytes 83886240 | tf_op jit(solution)/shard_map/snpa,sntb,snpxty->axby/dot_general | solution.py:58
  721.9 78.1 %bitcast_add_fusion = f32[16,256,8,256]{3,2,0,1:T(8,128)} fusion(f32[16,256,8,256]{3,2,1,0:T(8,128)} %param.8, f32[8,256,2,256,16]{3,4,2,1,0:T(8,128)} %fusion.20, s32[8,2]{0,1:T(2,128)S(1)} %copy.164), kind=kOutput, calls=%fused_computation.9 | convolution fusion | flops 1619001472 | bytes 134217792 | tf_op jit(solution)/shard_map/snpa,sntb,snpxty->axby/dot_general | solution.py:58
  799.9 12.2 slice.62
  816.7 94.5 %all-reduce.7.cloned.1.call-done = f32[16,256,256]{2,0,1:T(8,128)} async-done(((f32[16,256,256]{2,0,1:T(8,128)}), f32[16,256,256]{2,0,1:T(8,128)}) %all-reduce.7.cloned.1.call-update) | async-done | bytes 4194320 | tf_op jit(solution)/shard_map/psum | solution.py:11
  920.1 42.7 %all-reduce.9.cloned.1.call-done = f32[256,256]{1,0:T(8,128)} async-done(((f32[256,256]{1,0:T(8,128)}), f32[256,256]{1,0:T(8,128)}) %all-reduce.9.cloned.1.call-update) | async-done | bytes 262160 | tf_op jit(solution)/shard_map/psum | solution.py:11
  962.8 10.3 broadcast_select_fusion.2
  973.2 96.6 %all-reduce.11.cloned.1.call-done = f32[16,256,256]{2,0,1:T(8,128)} async-done(((f32[16,256,256]{2,0,1:T(8,128)}), f32[16,256,256]{2,0,1:T(8,128)}) %all-reduce.11.cloned.1.call-update) | async-done | bytes 4194320 | tf_op jit(solution)/shard_map/psum | solution.py:11
  1078.3 43.1 %all-reduce.13.cloned.1.call-done = f32[256,256]{1,0:T(8,128)} async-done(((f32[256,256]{1,0:T(8,128)}), f32[256,256]{1,0:T(8,128)}) %all-reduce.13.cloned.1.call-update) | async-done | bytes 262160 | tf_op jit(solution)/shard_map/psum | solution.py:11
  1121.4 8.9 fusion.9
  1130.6 96.4 %all-reduce.15.cloned.1.call-done = f32[16,256,256]{2,0,1:T(8,128)} async-done(((f32[16,256,256]{2,0,1:T(8,128)}), f32[16,256,256]{2,0,1:T(8,128)}) %all-reduce.15.cloned.1.call-update) | async-done | bytes 4194320 | tf_op jit(solution)/shard_map/psum | solution.py:11
  1239.4 15.1 reshape.317
  1275.3 131.5 %all-reduce.17.cloned.1.call-done = f32[8,256,768]{2,1,0:T(8,128)} async-done(((f32[8,256,768]{2,1,0:T(8,128)}), f32[8,256,768]{2,1,0:T(8,128)}) %all-reduce.17.cloned.1.call-update) | async-done | bytes 6291472 | tf_op jit(solution)/shard_map/psum | solution.py:11
  1406.8 86.7 %fusion.5 = f32[16,256,8,256]{3,0,2,1:T(8,128)} fusion(f32[8,256,768]{2,1,0:T(8,128)} %all-reduce.17.cloned.1.call-done, f32[16,256,256]{2,0,1:T(8,128)} %copy-done.7, f32[16,256,256]{2,0,1:T(8,128)} %copy-done.3, f32[16,256,256]{2,0,1:T(8,128)} %copy-done.5), kind=kOutput, calls=%fused_computation.16 | convolution fusion | flops 77315702784 | bytes 52428800 | tf_op jit(solution)/shard_map/axk,byk->axby/dot_general | solution.py:82
  1493.5 38.4 %subtract_select_fusion = f32[16,256,8,256]{3,2,0,1:T(8,128)} fusion(f32[16,256,8,256]{3,2,0,1:T(8,128)} %bitcast_add_fusion, f32[16,256,8,256]{3,0,2,1:T(8,128)} %fusion.5, pred[16,8]{1,0:T(8,128)(4,1)S(1)} %copy.148), kind=kLoop, calls=%fused_computation.8 | loop fusion | flops 16777216 | bytes 100663424 | tf_op jit(solution)/shard_map/jit(_where)/select_n | solution.py:91
  1531.9 15.2 broadcast_select_fusion.1
  1547.1 90.7 %scatter.4 = f32[16,256,8,256]{3,2,0,1:T(8,128)} dynamic-update-slice(f32[16,256,8,256]{3,2,0,1:T(8,128)} %subtract_select_fusion, f32[16,256,1,256]{3,2,0,1:T(1,128)} %broadcast_select_fusion.1, s32[]{:T(128)} %constant.195.clone.1, s32[]{:T(128)} %constant.195.clone.1, s32[]{:T(128)} %constant.195.clone.1, s32[]{:T(128)} %constant.195.clone.1) | dynamic-update-slice | bytes 8388612 | tf_op jit(solution)/shard_map/scatter | solution.py:97
  1637.8 22.9 %copy.178 = f32[16,256,8,256]{3,2,1,0:T(8,128)} copy(f32[16,256,8,256]{3,2,0,1:T(8,128)} %scatter.4) | data formatting | bytes 67108864 | tf_op jit(solution)/shard_map/scatter | solution.py:97
  (102 shorter events, 89.8 us)
Async XLA Ops:
  6.5 255.4 %copy-start = (s32[8]{0:T(128)S(1)}, s32[8]{0:T(128)}, u32[]{:S(2)}) copy-start(s32[8]{0:T(128)} %param.11) | copy-start | bytes 100
  38.4 190.7 %all-to-all-start = ((f32[2,4,4,256,512]{4,3,2,0,1:T(8,128)}), f32[2,4,4,256,512]{4,3,2,0,1:T(8,128)}, u32[]{:S(2)}, u32[]{:S(2)}) async-start(f32[2,4,4,256,512]{4,3,2,0,1:T(8,128)} %copy.156), calls=%async_computation | async-start | bytes 33554432 | tf_op jit(solution)/shard_map/all_to_all | solution.py:40
  255.6 7.4 copy-start.2
  255.6 369.6 %all-to-all-start.1 = ((f32[8,1,4,256,512]{4,3,2,1,0:T(8,128)}), f32[8,1,4,256,512]{4,3,2,1,0:T(8,128)}, u32[]{:S(2)}, u32[]{:S(2)}) async-start(f32[8,1,4,256,512]{4,3,2,1,0:T(8,128)} %fusion.2), calls=%async_computation.1 | async-start | bytes 33554432 | tf_op jit(solution)/shard_map/all_to_all | solution.py:48
  261.5 649.7 %all-reduce.7.cloned.1.call-start = ((), (), s32[]{:S(2)}) async-start(), calls=%async_computation.2 | async-start | bytes 8388608 | tf_op jit(solution)/shard_map/psum | solution.py:11
  812.2 1.9 copy-start.8
  816.6 94.6 %copy-start.9 = (f32[3,256,256]{2,1,0:T(8,128)S(1)}, f32[3,256,256]{2,1,0:T(8,128)}, u32[]{:S(2)}) copy-start(f32[3,256,256]{2,1,0:T(8,128)} %param.12) | copy-start | bytes 2359300
  816.6 146.2 %all-reduce.9.cloned.1.call-start = ((), (), s32[]{:S(2)}) async-start(), calls=%async_computation.3 | async-start | bytes 524288 | tf_op jit(solution)/shard_map/psum | solution.py:11
  916.6 2.0 copy-start.5
  919.6 150.1 %all-reduce.11.cloned.1.call-start = ((), (), s32[]{:S(2)}) async-start(), calls=%async_computation.4 | async-start | bytes 8388608 | tf_op jit(solution)/shard_map/psum | solution.py:11
  973.1 148.3 %all-reduce.13.cloned.1.call-start = ((), (), s32[]{:S(2)}) async-start(), calls=%async_computation.5 | async-start | bytes 524288 | tf_op jit(solution)/shard_map/psum | solution.py:11
  1075.2 2.1 copy-start.3
  1078.3 148.7 %all-reduce.15.cloned.1.call-start = ((), (), s32[]{:S(2)}) async-start(), calls=%async_computation.6 | async-start | bytes 8388608 | tf_op jit(solution)/shard_map/psum | solution.py:11
  1130.4 276.5 %all-reduce.17.cloned.1.call-start = ((), (), s32[]{:S(2)}) async-start(), calls=%async_computation.7 | async-start | bytes 12582912 | tf_op jit(solution)/shard_map/psum | solution.py:11
  1227.0 7.5 copy-start.4
  1227.0 7.5 copy-start.6
  1232.6 1.9 copy-start.7
  1268.2 0.8 copy-start.10
  1637.8 22.9 %copy-start.1 = (s32[8]{0:T(128)S(1)}, s32[8]{0:T(128)}, u32[]{:S(2)}) copy-start(s32[8]{0:T(128)} %param.11) | copy-start | bytes 100
Sparse Core Ops, SparseCore 0:
  816.7 94.4 all-reduce.6
  919.8 42.9 all-reduce.8
  973.2 96.5 all-reduce.10
  1078.4 42.9 all-reduce.12
  1130.5 96.4 all-reduce.14
  1268.3 138.4 all-reduce.16
where the time goes:
time: 1680 us; the launch traced here: 1670 us
  waiting for transfers between devices  1050 us (62%)
  matrix products  260 us (15%)
  local copies, waits for them, and re-layouts  238 us (14%)
  other arithmetic  94.4 us (6%)
    psum x6, waiting for transfers between devices, from_root(): return lax.psum(block, axis)  505 us
    all_to_all x1, waiting for transfers between devices, shards(): lax.all_to_all(outgoing, 'col', split_axis=0, concat_axis=0, tiled=True)  360 us
    all_to_all x1, waiting for transfers between devices, shards(): lax.all_to_all(outgoing, 'row', split_axis=1, concat_axis=0, tiled=True)  183 us
    dot_general x2, matrix products, shards(): jnp.einsum('snpa,sntb,snpxty->axby', row_hits, col_hits, pieces, precisio...  138 us
    scatter x2, local copies, waits for them, and re-layouts, shards(): result = result.at[:, :, 0, :].set(first_col)  114 us
    dot_general x1, matrix products, shards(): trailing_sum = jnp.einsum('axk,byk->axby', lower, across, precision=precise)  86.7 us
    select_n x1, other arithmetic, shards(): jnp.where(trailing[:, None, :, None], summed_front - trailing_sum, summed...  38.4 us
  transfers between devices with their start and end apart: 8, of which 8 were waited for; matrix products, arithmetic and copies ran while one was open for 1% of the time, Pallas kernels for 0%

commit v1 on v0

v1 whole, which is shorter than its diff:
```python
import functools

import jax
import jax.numpy as jnp
from jax import lax
from jax.experimental import pallas as pl
from jax.experimental.pallas import tpu as pltpu
from jax.sharding import PartitionSpec as P

DEPTH = 4


def copy_kernel(order_ref, cols_ref, in_ref, out_ref):
    out_ref[...] = in_ref[...].reshape(out_ref.shape)


def pack_rows(blocks, order, cols, rows_n, tile):
    slots, kblocks, _, _ = blocks.shape
    per_row = kblocks // rows_n
    spec = pltpu.PrefetchScalarGridSpec(
        num_scalar_prefetch=2,
        grid=(rows_n, slots, per_row),
        in_specs=[pl.BlockSpec((1, 1, tile, tile), lambda r, s, p, o, c: (s, o[s * kblocks + r * per_row + p], 0, c[s]))],
        out_specs=pl.BlockSpec((1, 1, 1, tile, tile), lambda r, s, p, o, c: (r, s, p, 0, 0)),
    )
    return pl.pallas_call(
        copy_kernel,
        grid_spec=spec,
        out_shape=jax.ShapeDtypeStruct((rows_n, slots, per_row, tile, tile), blocks.dtype),
        name="pack_rows",
    )(order.reshape(-1), cols, blocks)


def pack_slots(blocks, order):
    shape = blocks.shape
    spec = pltpu.PrefetchScalarGridSpec(
        num_scalar_prefetch=2,
        grid=(shape[0],),
        in_specs=[pl.BlockSpec((1,) + shape[1:], lambda i, o, c: (o[i], 0, 0, 0))],
        out_specs=pl.BlockSpec((1,) + shape[1:], lambda i, o, c: (i, 0, 0, 0)),
    )
    return pl.pallas_call(
        copy_kernel,
        grid_spec=spec,
        out_shape=jax.ShapeDtypeStruct(shape, blocks.dtype),
        compiler_params=pltpu.CompilerParams(vmem_limit_bytes=24 << 20),
        name="pack_slots",
    )(order, order, blocks)


def event_copies(index, pieces, buf, sems, event_ref):
    lane = lax.rem(index, DEPTH)
    return [
        pltpu.make_async_copy(piece.at[event_ref[index]], buf.at[lane, t], sems.at[lane, t])
        for t, piece in enumerate(pieces)
    ]


def run_events(a, start_ref, event_ref, steps, pieces, buf, sems, add):
    total = start_ref[steps]

    @pl.when(a == 0)
    def _():
        for first in range(DEPTH):
            @pl.when(first < total)
            def _():
                for copy in event_copies(jnp.int32(first), pieces, buf, sems, event_ref):
                    copy.start()

    def body(index, carry):
        for copy in event_copies(index, pieces, buf, sems, event_ref):
            copy.wait()
        add(index, lax.rem(index, DEPTH))

        @pl.when(index + DEPTH < total)
        def _():
            for copy in event_copies(index + DEPTH, pieces, buf, sems, event_ref):
                copy.start()

        return carry

    lax.fori_loop(start_ref[a], start_ref[a + 1], body, 0)


def panel_kernel(steps, start_ref, event_ref, front_ref, piece_ref, out_ref, buf, sems):
    a = pl.program_id(0)
    out_ref[...] = front_ref[...]

    def add(index, lane):
        out_ref[0] = out_ref[0] + buf[lane, 0]

    run_events(a, start_ref, event_ref, steps, [piece_ref], buf, sems, add)


def panel_sum(first, start, events, piece):
    steps, tile, _ = first.shape
    spec = pltpu.PrefetchScalarGridSpec(
        num_scalar_prefetch=2,
        grid=(steps,),
        in_specs=[pl.BlockSpec((1, tile, tile), lambda a, s, e: (a, 0, 0)), pl.BlockSpec(memory_space=pl.ANY)],
        out_specs=pl.BlockSpec((1, tile, tile), lambda a, s, e: (a, 0, 0)),
        scratch_shapes=[pltpu.VMEM((DEPTH, 1, tile, tile), jnp.float32), pltpu.SemaphoreType.DMA((DEPTH, 1))],
    )
    return pl.pallas_call(
        functools.partial(panel_kernel, steps),
        grid_spec=spec,
        out_shape=jax.ShapeDtypeStruct(first.shape, jnp.float32),
        name="panel_sum",
    )(start, events, first, piece)


def halves(x):
    high = x.astype(jnp.bfloat16)
    return high, (x - high.astype(jnp.float32)).astype(jnp.bfloat16)


def dot3(left, right):
    def one(u, v):
        return lax.dot_general(u, v, (((1,), (1,)), ((), ())), preferred_element_type=jnp.float32)

    return one(left[0], right[0]) + (one(left[0], right[1]) + one(left[1], right[0]))


def final_kernel(sizes, place_ref, mask_ref, start_ref, event_ref, target_ref, *refs):
    steps, cols, tile, panel, rows_n, cols_n, parts = sizes
    front_ref, panel_ref, across_ref, top_ref, inv_ref = refs[:5]
    pieces = list(refs[5:5 + parts])
    out_ref, wide_hi, wide_lo, top_hi, top_lo, inv_hi, inv_lo, buf, sems = refs[5 + parts:]
    a = pl.program_id(0)
    my_row, my_col = place_ref[0], place_ref[1]

    def cut(j):
        return slice(j * tile, (j + 1) * tile)

    def factor(load, count, block):
        got = []
        for j in range(count):
            column = load(j)
            for i in range(j):
                column = column - dot3(got[i][1], (top_hi[j, i], top_lo[j, i]))
            value = dot3(halves(column), (inv_hi[j], inv_lo[j]))
            value = jnp.where(block >= j, value, jnp.zeros_like(value))
            got.append((value, halves(value)))
        return got

    @pl.when(a == 0)
    def _():
        for j in range(panel):
            inv_hi[j], inv_lo[j] = halves(inv_ref[j])
        for row in range(1, panel):
            for i, (_, pair) in enumerate(factor(lambda j: top_ref[row, :, cut(j)], row, row)):
                top_hi[row, i], top_lo[row, i] = pair

        def widen(b, carry):
            for j, (_, pair) in enumerate(factor(lambda j: across_ref[b, :, cut(j)], panel, b * cols_n + my_col)):
                wide_hi[b, :, cut(j)], wide_lo[b, :, cut(j)] = pair
            return carry

        lax.fori_loop(0, cols, widen, 0)

    mine = factor(lambda j: panel_ref[0, :, cut(j)], panel, a * rows_n + my_row)
    high = jnp.concatenate([pair[0] for _, pair in mine], axis=1)
    low = jnp.concatenate([pair[1] for _, pair in mine], axis=1)
    for b in range(cols):
        update = dot3((high, low), (wide_hi[b], wide_lo[b]))
        for h in range(0, tile, 128):
            block = front_ref[0, :, b, h:h + 128]
            out_ref[0, :, b, h:h + 128] = jnp.where(mask_ref[a * cols + b] > 0, block - update[:, h:h + 128], block)

    def add(index, lane):
        for t in range(parts):
            for b in range(cols):
                @pl.when(target_ref[index * parts + t] == b)
                def _():
                    out_ref[0, :, b, :] = out_ref[0, :, b, :] + buf[lane, t]

    run_events(a, start_ref, event_ref, steps, pieces, buf, sems, add)
    for j in range(panel):
        @pl.when(my_col == j)
        def _():
            out_ref[0, :, 0, :] = mine[j][0]


def final_step(front, panel_s, across_s, top_s, inverses, pieces, place, mask, start, events, targets, rows_n, cols_n):
    steps, tile, cols, _ = front.shape
    panel = inverses.shape[0]
    parts = len(pieces)
    whole = pl.BlockSpec(memory_space=pltpu.VMEM)
    spec = pltpu.PrefetchScalarGridSpec(
        num_scalar_prefetch=5,
        grid=(steps,),
        in_specs=[
            pl.BlockSpec((1, tile, cols, tile), lambda a, *_: (a, 0, 0, 0)),
            pl.BlockSpec((1, tile, panel * tile), lambda a, *_: (a, 0, 0)),
            whole,
            whole,
            whole,
        ] + [pl.BlockSpec(memory_space=pl.ANY)] * parts,
        out_specs=pl.BlockSpec((1, tile, cols, tile), lambda a, *_: (a, 0, 0, 0)),
        scratch_shapes=[
            pltpu.VMEM((cols, tile, panel * tile), jnp.bfloat16),
            pltpu.VMEM((cols, tile, panel * tile), jnp.bfloat16),
            pltpu.VMEM((panel, panel, tile, tile), jnp.bfloat16),
            pltpu.VMEM((panel, panel, tile, tile), jnp.bfloat16),
            pltpu.VMEM((panel, tile, tile), jnp.bfloat16),
            pltpu.VMEM((panel, tile, tile), jnp.bfloat16),
            pltpu.VMEM((DEPTH, parts, tile, tile), jnp.float32),
            pltpu.SemaphoreType.DMA((DEPTH, parts)),
        ],
    )
    sizes = (steps, cols, tile, panel, rows_n, cols_n, parts)
    return pl.pallas_call(
        functools.partial(final_kernel, sizes),
        grid_spec=spec,
        out_shape=jax.ShapeDtypeStruct(front.shape, jnp.float32),
        compiler_params=pltpu.CompilerParams(vmem_limit_bytes=52 << 20),
        cost_estimate=pl.CostEstimate(
            flops=6 * front.size * panel * tile, bytes_accessed=10 * front.size, transcendentals=0
        ),
        name="final_step",
    )(place, mask, start, events, targets, front, panel_s, across_s, top_s, inverses, *pieces)


def event_list(keys, steps):
    order = jnp.argsort(keys).astype(jnp.int32)
    start = jnp.sum(keys[None, :] < jnp.arange(steps + 1)[:, None], axis=1).astype(jnp.int32)
    return order, start


def shards(front, children, child_rows, owner_slots, inverses, pattern):
    rows_n = lax.axis_size("row")
    cols_n = lax.axis_size("col")
    my_row = lax.axis_index("row")
    my_col = lax.axis_index("col")
    local_rows, tile, local_cols, _ = front.shape
    slots_here, child_order, child_width = children.shape
    kblocks = child_order // tile
    per_row = kblocks // rows_n
    per_col = child_width // tile
    slot_total = child_rows.shape[0]
    per_dest = slot_total // cols_n
    panel = inverses.shape[0]

    position = jnp.arange(kblocks, dtype=jnp.int32)
    row_order = jnp.argsort(child_rows % rows_n * kblocks + position[None, :], axis=1).astype(jnp.int32)
    my_order = lax.dynamic_slice_in_dim(row_order, my_row * slots_here, slots_here, 0)
    my_rank = lax.dynamic_slice_in_dim(row_order, my_row * per_row, per_row, 1)
    row_blocks = jnp.take_along_axis(child_rows, my_rank, axis=1)
    col_blocks = child_rows.reshape(slot_total, cols_n, per_col)
    col_pick = jnp.argsort(col_blocks, axis=2).astype(jnp.int32)
    col_sorted = jnp.sort(col_blocks, axis=2)
    my_pick = lax.dynamic_slice(col_pick, (my_row * slots_here, my_col, 0), (slots_here, 1, per_col))[:, 0]
    slot_ids = jnp.arange(slot_total, dtype=jnp.int32)
    dest_by_src = jnp.transpose(col_blocks[:, :, 0] % cols_n)
    send_order = jnp.argsort(dest_by_src * slot_total + slot_ids[None, :], axis=1).astype(jnp.int32)
    my_send = lax.dynamic_index_in_dim(send_order, my_col, 0, keepdims=False)

    blocks_in = children.reshape(slots_here, kblocks, tile, child_width)
    pieces = []
    for t in range(per_col):
        outgoing = pack_rows(blocks_in, my_order, my_pick[:, t], rows_n, tile)
        arrived = lax.all_to_all(outgoing, "row", split_axis=0, concat_axis=0, tiled=True)
        arrived = arrived.reshape(slot_total, per_row, tile, tile)
        outgoing = pack_slots(arrived, my_send)
        landed = lax.all_to_all(outgoing, "col", split_axis=0, concat_axis=0, tiled=True)
        pieces.append(landed.reshape(slot_total * per_row, tile, tile))

    recv_slot = lax.dynamic_slice_in_dim(send_order, my_col * per_dest, per_dest, 1)
    src_ids = jnp.arange(cols_n, dtype=jnp.int32)
    got_rows = row_blocks[recv_slot] // rows_n
    got_cols = (col_sorted[recv_slot, src_ids[:, None]] // cols_n).astype(jnp.int32)
    live = (owner_slots[recv_slot] > 0)[:, :, None]
    keys = jnp.where(live, got_rows, local_rows).reshape(-1)
    panel_keys = jnp.where(live & (got_cols[:, :, :1] == 0), got_rows, local_rows).reshape(-1)
    events, start = event_list(keys, local_rows)
    panel_events, panel_start = event_list(panel_keys, local_rows)
    targets = got_cols.reshape(cols_n * per_dest, per_col)[events // per_row].reshape(-1)

    current = panel_sum(front[:, :, 0, :], panel_start, panel_events, pieces[0])
    spread = jnp.concatenate(
        [jnp.where(my_col == j, current, jnp.zeros_like(current)) for j in range(panel)], axis=2
    )
    panel_s = lax.psum(spread, "col")

    ratio = cols_n // rows_n
    split = panel_s.reshape(local_cols, ratio, tile, panel * tile)
    chosen = lax.dynamic_index_in_dim(split, my_col // rows_n, 1, keepdims=False)
    tops = jnp.stack(
        [jnp.where(my_row == i % rows_n, panel_s[i // rows_n], jnp.zeros_like(panel_s[0])) for i in range(panel)]
    )
    chosen = jnp.where(my_row == my_col % rows_n, chosen, jnp.zeros_like(chosen))
    across_s, top_s = lax.psum((chosen, tops), "row")

    row_ids = jnp.arange(local_rows, dtype=jnp.int32) * rows_n + my_row
    col_ids = jnp.arange(local_cols, dtype=jnp.int32) * cols_n + my_col
    mask = pattern.reshape(local_rows, rows_n, local_cols, cols_n)
    mask = lax.dynamic_index_in_dim(mask, my_row, 1, keepdims=False)
    mask = lax.dynamic_index_in_dim(mask, my_col, 2, keepdims=False)
    mask = (mask > 0) & (row_ids >= panel)[:, None] & (col_ids >= panel)[None, :]
    place = jnp.stack([my_row, my_col]).astype(jnp.int32)
    return final_step(
        front, panel_s, across_s, top_s, inverses, pieces, place,
        mask.astype(jnp.int32).reshape(-1), start, events, targets, rows_n, cols_n,
    )


def solution(mesh):
    return jax.shard_map(
        shards,
        mesh=mesh,
        in_specs=(P(None, "row", None, "col"), P("row", None, "col"), P(), P(), P(), P()),
        out_specs=P(None, "row", None, "col"),
        check_vma=False,
    )
```

time: 1680 us -> 1100 us (0.65)
  matrix products: 260 us -> 0 us
  local copies, waits for them, and re-layouts: 238 us -> 18.8 us
  waiting for transfers between devices: 1050 us -> 837 us
  Pallas kernels: 0 us -> 176 us
  other arithmetic: 94.4 us -> 24.1 us
    dot_general x8 -> x0, matrix products: 260 us -> none  [the longest x2 138 us: shards(): jnp.einsum('snpa,sntb,snpxty->axby', row_hits, col_hits, pieces, precisio...]
    all_to_all x1 -> x2, waiting for transfers between devices: 360 us -> 164 us  [shards(): lax.all_to_all(outgoing, 'col', split_axis=0, concat_axis=0, tiled=True)]
    pallas_call x0 -> x6, Pallas kernels: none -> 176 us  [the longest x1 111 us: final_step(): pl.pallas_call(functools.partial(final_kernel, sizes), grid_spec=spec, ou...]
    scatter x2 -> x0, local copies, waits for them, and re-layouts: 114 us -> none  [shards(): result = result.at[:, :, 0, :].set(first_col)]
    select_n x11 -> x8, other arithmetic: 81.8 us -> 11.1 us  [the longest x1 6.07 us: shards(): jnp.where(my_row == my_col % rows_n, chosen, jnp.zeros_like(chosen))]
    all_to_all x1 -> x2, waiting for transfers between devices: 183 us -> 154 us  [shards(): lax.all_to_all(outgoing, 'row', split_axis=0, concat_axis=0, tiled=True)]
    gather x7 -> x6, local copies, waits for them, and re-layouts: 30.8 us -> 2.51 us  [the longest x2 0.65 us: shards(): col_sorted[recv_slot, src_ids[:, None]] // cols_n]
    another operation x1, local copies, waits for them, and re-layouts: 19.8 us -> 0.13 us
  transfers between devices with their start and end apart: 8 -> 6, of which waited for: 8 -> 5; matrix products, arithmetic and copies ran while one was open for 1% -> 3% of each run, Pallas kernels for 0% -> 4%
where the time goes in v1:
time: 1100 us; the launch traced here: 1090 us
  waiting for transfers between devices  837 us (76%)
  Pallas kernels  176 us (16%)
  other arithmetic  24.1 us (2%)
  starting transfers between devices  21.7 us (2%)
  local copies, waits for them, and re-layouts  18.8 us (2%)
  between operations  13.8 us (1%)
    psum x1, waiting for transfers between devices, shards(): panel_s = lax.psum(spread, 'col')  343 us
    psum x1, waiting for transfers between devices, shards(): across_s, top_s = lax.psum((chosen, tops), 'row')  176 us
    all_to_all x2, waiting for transfers between devices, shards(): lax.all_to_all(outgoing, 'col', split_axis=0, concat_axis=0, tiled=True)  164 us
    all_to_all x2, waiting for transfers between devices, shards(): lax.all_to_all(outgoing, 'row', split_axis=0, concat_axis=0, tiled=True)  154 us
    pallas_call x1, Pallas kernels, final_step(): pl.pallas_call(functools.partial(final_kernel, sizes), grid_spec=spec, ou...  111 us
    pallas_call x2, Pallas kernels, pack_rows(): pl.pallas_call(copy_kernel, grid_spec=spec, out_shape=jax.ShapeDtypeStruc...  39.8 us
  transfers between devices with their start and end apart: 6, of which 5 were waited for; matrix products, arithmetic and copies ran while one was open for 3% of the time, Pallas kernels for 4%

profile of v1, /device:TPU:0, one launch (start us, length us, event | category | flops | bytes accessed | tf_op | source)
XLA Modules:
  0.0 1091.1 jit_solution(7509402216537454038)
XLA Ops:
  10.0 19.8 %pack_rows.2 = f32[4,2,4,256,256]{4,3,2,1,0:T(8,128)} custom-call(s32[32]{0:T(128)} %reshape.260.order_ref, s32[2]{0:T(128)} %get-tuple-element.21.cols_ref, f32[2,16,256,512]{3,2,1,0:T(8,128)} %bitcast.61), custom_call_target="tpu_custom_call" | custom-call | tf_op jit(solution)/shard_map/pack_rows/pallas_call | solution.py:26
  29.8 5.7 all-to-all-start
  36.4 92.9 %all-to-all-done = f32[4,2,4,256,256]{4,3,2,1,0:T(8,128)} async-done(((f32[4,2,4,256,256]{4,3,2,1,0:T(8,128)}), f32[4,2,4,256,256]{4,3,2,1,0:T(8,128)}, u32[]{:S(2)}, u32[]{:S(2)}) %all-to-all-start) | async-done | bytes 8388640 | tf_op jit(solution)/shard_map/all_to_all | solution.py:262
  129.3 6.3 pack_slots.2
  135.6 3.4 copy-done.3
  139.0 5.1 all-to-all-start.1
  144.2 19.9 %pack_rows.3 = f32[4,2,4,256,256]{4,3,2,1,0:T(8,128)} custom-call(s32[32]{0:T(128)} %reshape.260.order_ref, s32[2]{0:T(128)} %get-tuple-element.20.cols_ref, f32[2,16,256,512]{3,2,1,0:T(8,128)} %bitcast.62), custom_call_target="tpu_custom_call" | custom-call | tf_op jit(solution)/shard_map/pack_rows/pallas_call | solution.py:26
  164.1 164.1 %all-to-all-done.1 = f32[8,4,256,256]{3,2,1,0:T(8,128)} async-done(((f32[8,4,256,256]{3,2,1,0:T(8,128)}), f32[8,4,256,256]{3,2,1,0:T(8,128)}, u32[]{:S(2)}, u32[]{:S(2)}) %all-to-all-start.1) | async-done | bytes 8388640 | tf_op jit(solution)/shard_map/all_to_all | solution.py:265
  328.2 5.7 all-to-all-start.2
  337.5 2.2 slice-done
  339.7 2.4 copy.46
  342.1 1.7 sort.93
  344.5 12.3 %panel_sum.1 = f32[16,256,256]{2,1,0:T(8,128)} custom-call(s32[17]{0:T(128)} %convert_reduce_fusion.start_ref, s32[32]{0:T(128)} %get-tuple-element.18.event_ref, f32[16,256,256]{2,1,0:T(8,128)} %bitcast.63, f32[32,256,256]{2,1,0:T(8,128)} %bitcast.17.piece_ref.refs_5_), custom_call_target="tpu_custom_call" | custom-call | tf_op jit(solution)/shard_map/panel_sum/pallas_call | solution.py:104
  356.8 3.7 broadcast_select_fusion.2
  360.5 5.0 pad_maximum_fusion
  365.5 60.7 %all-to-all-done.2 = f32[4,2,4,256,256]{4,3,2,1,0:T(8,128)} async-done(((f32[4,2,4,256,256]{4,3,2,1,0:T(8,128)}), f32[4,2,4,256,256]{4,3,2,1,0:T(8,128)}, u32[]{:S(2)}, u32[]{:S(2)}) %all-to-all-start.2) | async-done | bytes 8388640 | tf_op jit(solution)/shard_map/all_to_all | solution.py:262
  426.2 6.4 pack_slots.3
  432.6 3.3 copy-done.2
  435.9 5.0 all-to-all-start.3
  441.2 342.7 %all-reduce.4.cloned.1.call-done.refs_1_ = f32[16,256,768]{2,1,0:T(8,128)} async-done(((f32[16,256,768]{2,1,0:T(8,128)}), f32[16,256,768]{2,1,0:T(8,128)}) %all-reduce.4.cloned.1.call-update) | async-done | bytes 12582928 | tf_op jit(solution)/shard_map/psum | solution.py:283
  786.9 6.1 fusion
  793.5 1.6 sort.91
  796.7 176.5 %all-reduce.6.cloned.1.call-done = (f32[8,256,768]{2,1,0:T(8,128)}, f32[3,256,768]{2,1,0:T(8,128)}) async-done(((f32[8,256,768]{2,1,0:T(8,128)}, f32[3,256,768]{2,1,0:T(8,128)}), (f32[8,256,768]{2,1,0:T(8,128)}, f32[3,256,768]{2,1,0:T(8,128)})) %all-reduce.6.cloned.1.call-update) | async-done | bytes 8650768 | tf_op jit(solution)/shard_map/psum | solution.py:292
  973.2 111.1 %final_step.1 = f32[16,256,8,256]{3,2,1,0:T(8,128)} custom-call(s32[2]{0:T(128)S(1)} %pad_add_fusion.place_ref, s32[128]{0:T(128)S(1)} %and_convert_fusion.mask_ref, s32[17]{0:T(128)S(1)} %convert_reduce_fusion.1.start_ref, s32[32]{0:T(128)S(1)} %get-tuple-element.16.event_ref, s32[64]{0:T(128)S(1)} %reshape.259.target_ref, f32[16,256,8,256]{3,2,1,0:T(8,128)} %refs_0_.1, ...), custom_call_target="tpu_custom_call" | custom-call | flops 38654705664 | bytes 83886080 | tf_op jit(solution)/shard_map/final_step/pallas_call | solution.py:212
  (88 shorter events, 13.8 us)
Async XLA Ops:
  6.5 328.5 %copy-start = (s32[8]{0:T(128)S(1)}, s32[8]{0:T(128)}, u32[]{:S(2)}) copy-start(s32[8]{0:T(128)} %param.9) | copy-start | bytes 100
  29.8 99.5 %all-to-all-start = ((f32[4,2,4,256,256]{4,3,2,1,0:T(8,128)}), f32[4,2,4,256,256]{4,3,2,1,0:T(8,128)}, u32[]{:S(2)}, u32[]{:S(2)}) async-start(f32[4,2,4,256,256]{4,3,2,1,0:T(8,128)} %pack_rows.2), calls=%async_computation | async-start | bytes 16777216 | tf_op jit(solution)/shard_map/all_to_all | solution.py:262
  135.6 3.4 copy-start.3
  139.0 189.1 %all-to-all-start.1 = ((f32[8,4,256,256]{3,2,1,0:T(8,128)}), f32[8,4,256,256]{3,2,1,0:T(8,128)}, u32[]{:S(2)}, u32[]{:S(2)}) async-start(f32[8,4,256,256]{3,2,1,0:T(8,128)} %copy-done.3), calls=%async_computation.1 | async-start | bytes 16777216 | tf_op jit(solution)/shard_map/all_to_all | solution.py:265
  164.1 170.2 %copy-start.5 = (s32[8,16]{1,0:T(8,128)S(1)}, s32[8,16]{1,0:T(8,128)}, u32[]{:S(2)}) copy-start(s32[8,16]{1,0:T(8,128)} %param.8) | copy-start | bytes 1540
  328.2 98.1 %all-to-all-start.2 = ((f32[4,2,4,256,256]{4,3,2,1,0:T(8,128)}), f32[4,2,4,256,256]{4,3,2,1,0:T(8,128)}, u32[]{:S(2)}, u32[]{:S(2)}) async-start(f32[4,2,4,256,256]{4,3,2,1,0:T(8,128)} %pack_rows.3), calls=%async_computation.2 | async-start | bytes 16777216 | tf_op jit(solution)/shard_map/all_to_all | solution.py:262
  333.8 450.1 %all-reduce.4.cloned.1.call-start = ((), (), s32[]{:S(2)}) async-start(), calls=%async_computation.4 | async-start | bytes 25165824 | tf_op jit(solution)/shard_map/psum | solution.py:283
  337.5 2.2 slice-start
  432.6 3.3 copy-start.2
  435.9 360.7 %all-to-all-start.3 = ((f32[8,4,256,256]{3,2,1,0:T(8,128)}), f32[8,4,256,256]{3,2,1,0:T(8,128)}, u32[]{:S(2)}, u32[]{:S(2)}) async-start(f32[8,4,256,256]{3,2,1,0:T(8,128)} %copy-done.2), calls=%async_computation.3 | async-start | bytes 16777216 | tf_op jit(solution)/shard_map/all_to_all | solution.py:265
  440.9 532.2 %all-reduce.6.cloned.1.call-start = ((), (), s32[]{:S(2)}) async-start(), calls=%async_computation.5 | async-start | bytes 17301504 | tf_op jit(solution)/shard_map/psum | solution.py:292
  792.9 2.9 copy-start.6
  792.9 180.3 %copy-start.4 = (f32[3,256,256]{2,1,0:T(8,128)S(1)}, f32[3,256,256]{2,1,0:T(8,128)}, u32[]{:S(2)}) copy-start(f32[3,256,256]{2,1,0:T(8,128)} %refs_4_.1) | copy-start | bytes 2359300
  973.2 111.1 %copy-start.1 = (s32[8]{0:T(128)S(1)}, s32[8]{0:T(128)}, u32[]{:S(2)}) copy-start(s32[8]{0:T(128)} %param.9) | copy-start | bytes 100
Sparse Core Ops, SparseCore 0:
  365.6 418.2 all-reduce.3
  793.1 180.0 all-reduce.5

commit v2 on v1

--- a/solution.py
+++ b/solution.py
@@ -123,9 +123,11 @@
 
 def final_kernel(sizes, place_ref, mask_ref, start_ref, event_ref, target_ref, *refs):
     steps, cols, tile, panel, rows_n, cols_n, parts = sizes
-    front_ref, panel_ref, across_ref, top_ref, inv_ref = refs[:5]
-    pieces = list(refs[5:5 + parts])
-    out_ref, wide_hi, wide_lo, top_hi, top_lo, inv_hi, inv_lo, buf, sems = refs[5 + parts:]
+    front_ref, top_ref, inv_ref = refs[:3]
+    panel_refs = refs[3:3 + panel]
+    across_refs = refs[3 + panel:3 + 2 * panel]
+    pieces = list(refs[3 + 2 * panel:3 + 2 * panel + parts])
+    out_ref, wide_hi, wide_lo, top_hi, top_lo, inv_hi, inv_lo, buf, sems = refs[3 + 2 * panel + parts:]
     a = pl.program_id(0)
     my_row, my_col = place_ref[0], place_ref[1]
 
@@ -152,13 +154,13 @@
                 top_hi[row, i], top_lo[row, i] = pair
 
         def widen(b, carry):
-            for j, (_, pair) in enumerate(factor(lambda j: across_ref[b, :, cut(j)], panel, b * cols_n + my_col)):
+            for j, (_, pair) in enumerate(factor(lambda j: across_refs[j][b], panel, b * cols_n + my_col)):
                 wide_hi[b, :, cut(j)], wide_lo[b, :, cut(j)] = pair
             return carry
 
         lax.fori_loop(0, cols, widen, 0)
 
-    mine = factor(lambda j: panel_ref[0, :, cut(j)], panel, a * rows_n + my_row)
+    mine = factor(lambda j: panel_refs[j][0], panel, a * rows_n + my_row)
     high = jnp.concatenate([pair[0] for _, pair in mine], axis=1)
     low = jnp.concatenate([pair[1] for _, pair in mine], axis=1)
     for b in range(cols):
@@ -191,11 +193,9 @@
         grid=(steps,),
         in_specs=[
             pl.BlockSpec((1, tile, cols, tile), lambda a, *_: (a, 0, 0, 0)),
-            pl.BlockSpec((1, tile, panel * tile), lambda a, *_: (a, 0, 0)),
             whole,
             whole,
-            whole,
-        ] + [pl.BlockSpec(memory_space=pl.ANY)] * parts,
+        ] + [pl.BlockSpec((1, tile, tile), lambda a, *_: (a, 0, 0))] * panel + [whole] * panel + [pl.BlockSpec(memory_space=pl.ANY)] * parts,
         out_specs=pl.BlockSpec((1, tile, cols, tile), lambda a, *_: (a, 0, 0, 0)),
         scratch_shapes=[
             pltpu.VMEM((cols, tile, panel * tile), jnp.bfloat16),
@@ -218,13 +218,33 @@
             flops=6 * front.size * panel * tile, bytes_accessed=10 * front.size, transcendentals=0
         ),
         name="final_step",
-    )(place, mask, start, events, targets, front, panel_s, across_s, top_s, inverses, *pieces)
+    )(place, mask, start, events, targets, front, top_s, inverses, *panel_s, *across_s, *pieces)
 
 
 def event_list(keys, steps):
     order = jnp.argsort(keys).astype(jnp.int32)
     start = jnp.sum(keys[None, :] < jnp.arange(steps + 1)[:, None], axis=1).astype(jnp.int32)
     return order, start
+
+
+def row_spread(block, rows_n, cols_n, my_row, my_col):
+    half = block.shape[0] // 2
+    steps = [1 << k for k in range((rows_n - 1).bit_length())]
+    apart = my_row ^ (my_col % rows_n)
+    done = []
+    for part, order in ((block[:half], steps), (block[half:], steps[::-1])):
+        held = [0]
+        for step in order:
+            pairs = [
+                (((c % rows_n) ^ h) * cols_n + c, ((c % rows_n) ^ h ^ step) * cols_n + c)
+                for c in range(cols_n) for h in held
+            ]
+            came = lax.ppermute(part, ("row", "col"), pairs)
+            fresh = functools.reduce(jnp.logical_or, [apart == (h ^ step) for h in held])
+            part = jnp.where(fresh, came, part)
+            held = held + [h ^ step for h in held]
+        done.append(part)
+    return jnp.concatenate(done, axis=0)
 
 
 def shards(front, children, child_rows, owner_slots, inverses, pattern):
@@ -277,19 +297,23 @@
     targets = got_cols.reshape(cols_n * per_dest, per_col)[events // per_row].reshape(-1)
 
     current = panel_sum(front[:, :, 0, :], panel_start, panel_events, pieces[0])
-    spread = jnp.concatenate(
-        [jnp.where(my_col == j, current, jnp.zeros_like(current)) for j in range(panel)], axis=2
-    )
-    panel_s = lax.psum(spread, "col")
-
     ratio = cols_n // rows_n
-    split = panel_s.reshape(local_cols, ratio, tile, panel * tile)
-    chosen = lax.dynamic_index_in_dim(split, my_col // rows_n, 1, keepdims=False)
-    tops = jnp.stack(
-        [jnp.where(my_row == i % rows_n, panel_s[i // rows_n], jnp.zeros_like(panel_s[0])) for i in range(panel)]
-    )
-    chosen = jnp.where(my_row == my_col % rows_n, chosen, jnp.zeros_like(chosen))
-    across_s, top_s = lax.psum((chosen, tops), "row")
+    panel_s, across_s = [], []
+    for j in range(panel):
+        column = lax.psum(jnp.where(my_col == j, current, jnp.zeros_like(current)), "col")
+        current, column = lax.optimization_barrier((current, column))
+        split = column.reshape(local_cols, ratio, tile, tile)
+        chosen = lax.dynamic_index_in_dim(split, my_col // rows_n, 1, keepdims=False)
+        panel_s.append(column)
+        across_s.append(row_spread(chosen, rows_n, cols_n, my_row, my_col))
+    tops = jnp.stack([
+        jnp.concatenate([
+            jnp.where(my_row == i % rows_n, panel_s[j][i // rows_n], jnp.zeros_like(panel_s[0][0]))
+            for j in range(panel - 1)
+        ], axis=1)
+        for i in range(panel)
+    ])
+    top_s = lax.psum(tops, "row")
 
     row_ids = jnp.arange(local_rows, dtype=jnp.int32) * rows_n + my_row
     col_ids = jnp.arange(local_cols, dtype=jnp.int32) * cols_n + my_col

time: 1100 us -> 1090 us (level)
  waiting for transfers between devices: 837 us -> 798 us
  starting transfers between devices: 21.7 us -> 52.8 us
    psum x2 -> x4, waiting for transfers between devices: 519 us -> 386 us  [the longest x3 386 us: shards(): lax.psum(jnp.where(my_col == j, current, jnp.zeros_like(current)), 'col')]
    ppermute x0 -> x12, waiting for transfers between devices: none -> 81.7 us  [row_spread(): came = lax.ppermute(part, ('row', 'col'), pairs)]
    ppermute x0 -> x12, starting transfers between devices: none -> 31.3 us  [row_spread(): came = lax.ppermute(part, ('row', 'col'), pairs)]
  transfers between devices with their start and end apart: 6 -> 20, of which waited for: 5 -> 11; matrix products, arithmetic and copies ran while one was open for 3% -> 3% of each run, Pallas kernels for 4% -> 4%
where the time goes in v2:
time: 1090 us
  waiting for transfers between devices  798 us (73%)
  Pallas kernels  177 us (16%)
  starting transfers between devices  52.8 us (5%)
  other arithmetic  27.9 us (3%)
  local copies, waits for them, and re-layouts  22.5 us (2%)
  between operations  13.8 us (1%)
    psum x3, waiting for transfers between devices, shards(): lax.psum(jnp.where(my_col == j, current, jnp.zeros_like(current)), 'col')  386 us
    all_to_all x2, waiting for transfers between devices, shards(): lax.all_to_all(outgoing, 'col', split_axis=0, concat_axis=0, tiled=True)  174 us
    all_to_all x2, waiting for transfers between devices, shards(): lax.all_to_all(outgoing, 'row', split_axis=0, concat_axis=0, tiled=True)  155 us
    pallas_call x1, Pallas kernels, final_step(): pl.pallas_call(functools.partial(final_kernel, sizes), grid_spec=spec, ou...  113 us
    ppermute x12, waiting for transfers between devices, row_spread(): came = lax.ppermute(part, ('row', 'col'), pairs)  81.7 us
    pallas_call x2, Pallas kernels, pack_rows(): pl.pallas_call(copy_kernel, grid_spec=spec, out_shape=jax.ShapeDtypeStruc...  39.7 us
    ppermute x12, starting transfers between devices, row_spread(): came = lax.ppermute(part, ('row', 'col'), pairs)  31.3 us
  transfers between devices with their start and end apart: 20, of which 11 were waited for; matrix products, arithmetic and copies ran while one was open for 3% of the time, Pallas kernels for 4%

profile of v2, /device:TPU:0, one launch (start us, length us, event | category | flops | bytes accessed | tf_op | source)
XLA Modules:
  0.0 1091.6 jit_solution(4777469788459835551)
XLA Ops:
  10.0 19.8 %pack_rows.2 = f32[4,2,4,256,256]{4,3,2,1,0:T(8,128)} custom-call(s32[32]{0:T(128)} %reshape.287.order_ref, s32[2]{0:T(128)} %get-tuple-element.31.cols_ref, f32[2,16,256,512]{3,2,1,0:T(8,128)} %bitcast.102), custom_call_target="tpu_custom_call" | custom-call | tf_op jit(solution)/shard_map/pack_rows/pallas_call | solution.py:26
  29.8 5.7 all-to-all-start
  35.5 19.9 %pack_rows.3 = f32[4,2,4,256,256]{4,3,2,1,0:T(8,128)} custom-call(s32[32]{0:T(128)} %reshape.287.order_ref, s32[2]{0:T(128)} %get-tuple-element.30.cols_ref, f32[2,16,256,512]{3,2,1,0:T(8,128)} %bitcast.103), custom_call_target="tpu_custom_call" | custom-call | tf_op jit(solution)/shard_map/pack_rows/pallas_call | solution.py:26
  55.4 73.9 %all-to-all-done = f32[4,2,4,256,256]{4,3,2,1,0:T(8,128)} async-done(((f32[4,2,4,256,256]{4,3,2,1,0:T(8,128)}), f32[4,2,4,256,256]{4,3,2,1,0:T(8,128)}, u32[]{:S(2)}, u32[]{:S(2)}) %all-to-all-start) | async-done | bytes 8388640 | tf_op jit(solution)/shard_map/all_to_all | solution.py:282
  129.3 5.7 all-to-all-start.2
  135.9 6.3 pack_slots.2
  145.6 81.4 %all-to-all-done.2 = f32[4,2,4,256,256]{4,3,2,1,0:T(8,128)} async-done(((f32[4,2,4,256,256]{4,3,2,1,0:T(8,128)}), f32[4,2,4,256,256]{4,3,2,1,0:T(8,128)}, u32[]{:S(2)}, u32[]{:S(2)}) %all-to-all-start.2) | async-done | bytes 8388640 | tf_op jit(solution)/shard_map/all_to_all | solution.py:282
  227.0 5.0 all-to-all-start.1
  232.0 6.3 pack_slots.3
  241.5 174.4 %all-to-all-done.1 = f32[8,4,256,256]{3,2,1,0:T(8,128)} async-done(((f32[8,4,256,256]{3,2,1,0:T(8,128)}), f32[8,4,256,256]{3,2,1,0:T(8,128)}, u32[]{:S(2)}, u32[]{:S(2)}) %all-to-all-start.1) | async-done | bytes 8388640 | tf_op jit(solution)/shard_map/all_to_all | solution.py:285
  415.9 5.0 all-to-all-start.3
  431.5 11.9 %panel_sum.1 = f32[16,256,256]{2,1,0:T(8,128)} custom-call(s32[17]{0:T(128)} %convert_reduce_fusion.start_ref, s32[32]{0:T(128)} %get-tuple-element.23.event_ref, f32[16,256,256]{2,1,0:T(8,128)} %bitcast.104, f32[32,256,256]{2,1,0:T(8,128)} %bitcast.17.piece_ref.refs_9_), custom_call_target="tpu_custom_call" | custom-call | tf_op jit(solution)/shard_map/panel_sum/pallas_call | solution.py:104
  443.4 4.6 broadcast_select_fusion.2
  448.1 233.9 %all-reduce.5.cloned.1.call-done.refs_3_ = f32[16,256,256]{2,1,0:T(8,128)} async-done(((f32[16,256,256]{2,1,0:T(8,128)}), f32[16,256,256]{2,1,0:T(8,128)}) %all-reduce.5.cloned.1.call-update) | async-done | bytes 4194320 | tf_op jit(solution)/shard_map/psum | solution.py:303
  695.4 85.2 %all-reduce.7.cloned.1.call-done.refs_4_ = f32[16,256,256]{2,1,0:T(8,128)} async-done(((f32[16,256,256]{2,1,0:T(8,128)}), f32[16,256,256]{2,1,0:T(8,128)}) %all-reduce.7.cloned.1.call-update) | async-done | bytes 4194320 | tf_op jit(solution)/shard_map/psum | solution.py:303
  785.6 4.3 collective-permute-start.1
  790.0 4.3 collective-permute-start.3
  800.7 10.8 collective-permute-done.1
  814.0 67.0 %all-reduce.11.cloned.1.call-done.refs_5_ = f32[16,256,256]{2,1,0:T(8,128)} async-done(((f32[16,256,256]{2,1,0:T(8,128)}), f32[16,256,256]{2,1,0:T(8,128)}) %all-reduce.11.cloned.1.call-update) | async-done | bytes 4194320 | tf_op jit(solution)/shard_map/psum | solution.py:303
  894.3 12.6 %collective-permute-done.8 = f32[4,256,256]{2,1,0:T(8,128)S(1)} collective-permute-done((f32[4,256,256]{2,1,0:T(8,128)S(1)}, f32[4,256,256]{2,1,0:T(8,128)S(1)}, u32[]{:S(2)}, u32[]{:S(2)}) %collective-permute-start.8) | collective-permute-done | bytes 1048608 | tf_op jit(solution)/shard_map/ppermute | solution.py:242
  908.5 15.2 %collective-permute-done.10 = f32[4,256,256]{2,1,0:T(8,128)S(1)} collective-permute-done((f32[4,256,256]{2,1,0:T(8,128)S(1)}, f32[4,256,256]{2,1,0:T(8,128)S(1)}, u32[]{:S(2)}, u32[]{:S(2)}) %collective-permute-start.10) | collective-permute-done | bytes 1048608 | tf_op jit(solution)/shard_map/ppermute | solution.py:242
  925.3 25.0 %collective-permute-done.5 = f32[4,256,256]{2,1,0:T(8,128)S(1)} collective-permute-done((f32[4,256,256]{2,1,0:T(8,128)S(1)}, f32[4,256,256]{2,1,0:T(8,128)S(1)}, u32[]{:S(2)}, u32[]{:S(2)}) %collective-permute-start.5) | collective-permute-done | bytes 1048608 | tf_op jit(solution)/shard_map/ppermute | solution.py:242
  952.1 18.1 %collective-permute-done.9 = f32[4,256,256]{2,1,0:T(8,128)S(1)} collective-permute-done((f32[4,256,256]{2,1,0:T(8,128)S(1)}, f32[4,256,256]{2,1,0:T(8,128)S(1)}, u32[]{:S(2)}, u32[]{:S(2)}) %collective-permute-start.9) | collective-permute-done | bytes 1048608 | tf_op jit(solution)/shard_map/ppermute | solution.py:242
  972.1 112.9 %final_step.1 = f32[16,256,8,256]{3,2,1,0:T(8,128)} custom-call(s32[2]{0:T(128)S(1)} %pad_add_fusion.place_ref, s32[128]{0:T(128)S(1)} %and_convert_fusion.mask_ref, s32[17]{0:T(128)S(1)} %convert_reduce_fusion.1.start_ref, s32[32]{0:T(128)S(1)} %get-tuple-element.21.event_ref, s32[64]{0:T(128)S(1)} %reshape.286.target_ref, f32[16,256,8,256]{3,2,1,0:T(8,128)} %refs_0_.1, ...), custom_call_target="tpu_custom_call" | custom-call | flops 38654705664 | bytes 83886080 | tf_op jit(solution)/shard_map/final_step/pallas_call | solution.py:212
  (143 shorter events, 68.7 us)
Async XLA Ops:
  6.5 415.7 %copy-start = (s32[8]{0:T(128)S(1)}, s32[8]{0:T(128)}, u32[]{:S(2)}) copy-start(s32[8]{0:T(128)} %param.9) | copy-start | bytes 100
  29.8 99.5 %all-to-all-start = ((f32[4,2,4,256,256]{4,3,2,1,0:T(8,128)}), f32[4,2,4,256,256]{4,3,2,1,0:T(8,128)}, u32[]{:S(2)}, u32[]{:S(2)}) async-start(f32[4,2,4,256,256]{4,3,2,1,0:T(8,128)} %pack_rows.2), calls=%async_computation | async-start | bytes 16777216 | tf_op jit(solution)/shard_map/all_to_all | solution.py:282
  129.3 97.7 %all-to-all-start.2 = ((f32[4,2,4,256,256]{4,3,2,1,0:T(8,128)}), f32[4,2,4,256,256]{4,3,2,1,0:T(8,128)}, u32[]{:S(2)}, u32[]{:S(2)}) async-start(f32[4,2,4,256,256]{4,3,2,1,0:T(8,128)} %pack_rows.3), calls=%async_computation.2 | async-start | bytes 16777216 | tf_op jit(solution)/shard_map/all_to_all | solution.py:282
  227.0 188.9 %all-to-all-start.1 = ((f32[8,4,256,256]{3,2,1,0:T(8,128)}), f32[8,4,256,256]{3,2,1,0:T(8,128)}, u32[]{:S(2)}, u32[]{:S(2)}) async-start(f32[8,4,256,256]{3,2,1,0:T(8,128)} %copy-done.3), calls=%async_computation.1 | async-start | bytes 16777216 | tf_op jit(solution)/shard_map/all_to_all | solution.py:285
  241.5 179.9 %copy-start.5 = (s32[8,16]{1,0:T(8,128)S(1)}, s32[8,16]{1,0:T(8,128)}, u32[]{:S(2)}) copy-start(s32[8,16]{1,0:T(8,128)} %param.8) | copy-start | bytes 1540
  415.9 556.2 %all-to-all-start.3 = ((f32[8,4,256,256]{3,2,1,0:T(8,128)}), f32[8,4,256,256]{3,2,1,0:T(8,128)}, u32[]{:S(2)}, u32[]{:S(2)}) async-start(f32[8,4,256,256]{3,2,1,0:T(8,128)} %copy-done.2), calls=%async_computation.3 | async-start | bytes 16777216 | tf_op jit(solution)/shard_map/all_to_all | solution.py:285
  421.0 261.0 %all-reduce.5.cloned.1.call-start = ((), (), s32[]{:S(2)}) async-start(), calls=%async_computation.4 | async-start | bytes 8388608 | tf_op jit(solution)/shard_map/psum | solution.py:303
  448.0 332.5 %all-reduce.7.cloned.1.call-start = ((), (), s32[]{:S(2)}) async-start(), calls=%async_computation.5 | async-start | bytes 8388608 | tf_op jit(solution)/shard_map/psum | solution.py:303
  684.4 196.5 %all-reduce.11.cloned.1.call-start = ((), (), s32[]{:S(2)}) async-start(), calls=%async_computation.7 | async-start | bytes 8388608 | tf_op jit(solution)/shard_map/psum | solution.py:303
  689.9 94.5 %collective-permute-start = (f32[4,256,256]{2,1,0:T(8,128)S(1)}, f32[4,256,256]{2,1,0:T(8,128)S(1)}, u32[]{:S(2)}, u32[]{:S(2)}) collective-permute-start(f32[4,256,256]{2,1,0:T(8,128)S(1)} %get-tuple-element.38), channel_id=1, source_target_pairs={{0,8},{9,1},{18,26},{27,19},{4,12},{13,5},{22,30},{31,23}} | collective-permute-start | bytes 3145736 | tf_op jit(solution)/shard_map/ppermute | solution.py:242
  693.1 96.8 %collective-permute-start.2 = (f32[4,256,256]{2,1,0:T(8,128)S(1)}, f32[4,256,256]{2,1,0:T(8,128)}, u32[]{:S(2)}, u32[]{:S(2)}) collective-permute-start(f32[4,256,256]{2,1,0:T(8,128)S(1)} %get-tuple-element.39), channel_id=1, source_target_pairs={{0,16},{9,25},{18,2},{27,11},{4,20},{13,29},{22,6},{31,15}} | collective-permute-start | bytes 3145736 | tf_op jit(solution)/shard_map/ppermute | solution.py:242
  783.0 189.1 %all-reduce.9.cloned.1.call-start = ((), (), s32[]{:S(2)}) async-start(), calls=%async_computation.6 | async-start | bytes 3145728 | tf_op jit(solution)/shard_map/psum | solution.py:316
  783.1 11.3 %copy-start.7 = (f32[16,256,256]{2,1,0:T(8,128)S(1)}, f32[16,256,256]{2,1,0:T(8,128)}, u32[]{:S(2)}) copy-start(f32[16,256,256]{2,1,0:T(8,128)} %all-reduce.7.cloned.1.call-done.refs_4_) | copy-start | bytes 12582916
  785.6 26.0 %collective-permute-start.1 = (f32[4,256,256]{2,1,0:T(8,128)}, f32[4,256,256]{2,1,0:T(8,128)}, u32[]{:S(2)}, u32[]{:S(2)}) collective-permute-start(f32[4,256,256]{2,1,0:T(8,128)} %broadcast_select_fusion.11), channel_id=1, source_target_pairs={{0,16},{8,24},{9,25},{1,17},{18,2},{26,10},{27,11},{19,3},{4,20},{... | collective-permute-start | bytes 3145736 | tf_op jit(solution)/shard_map/ppermute | solution.py:242
  790.0 96.3 %collective-permute-start.3 = (f32[4,256,256]{2,1,0:T(8,128)S(1)}, f32[4,256,256]{2,1,0:T(8,128)}, u32[]{:S(2)}, u32[]{:S(2)}) collective-permute-start(f32[4,256,256]{2,1,0:T(8,128)S(1)} %broadcast_select_fusion.5), channel_id=1, source_target_pairs={{0,8},{16,24},{9,1},{25,17},{18,26},{2,10},{27,19},{11,3},{4,12},{... | collective-permute-start | bytes 3145736 | tf_op jit(solution)/shard_map/ppermute | solution.py:242
  794.6 93.2 %collective-permute-start.4 = (f32[4,256,256]{2,1,0:T(8,128)S(1)}, f32[4,256,256]{2,1,0:T(8,128)}, u32[]{:S(2)}, u32[]{:S(2)}) collective-permute-start(f32[4,256,256]{2,1,0:T(8,128)S(1)} %get-tuple-element.36), channel_id=1, source_target_pairs={{0,8},{9,1},{18,26},{27,19},{4,12},{13,5},{22,30},{31,23}} | collective-permute-start | bytes 3145736 | tf_op jit(solution)/shard_map/ppermute | solution.py:242
  796.9 92.4 %collective-permute-start.6 = (f32[4,256,256]{2,1,0:T(8,128)S(1)}, f32[4,256,256]{2,1,0:T(8,128)}, u32[]{:S(2)}, u32[]{:S(2)}) collective-permute-start(f32[4,256,256]{2,1,0:T(8,128)S(1)} %get-tuple-element.37), channel_id=1, source_target_pairs={{0,16},{9,25},{18,2},{27,11},{4,20},{13,29},{22,6},{31,15}} | collective-permute-start | bytes 3145736 | tf_op jit(solution)/shard_map/ppermute | solution.py:242
  882.7 24.2 %collective-permute-start.8 = (f32[4,256,256]{2,1,0:T(8,128)S(1)}, f32[4,256,256]{2,1,0:T(8,128)S(1)}, u32[]{:S(2)}, u32[]{:S(2)}) collective-permute-start(f32[4,256,256]{2,1,0:T(8,128)S(1)} %get-tuple-element.34), channel_id=1, source_target_pairs={{0,8},{9,1},{18,26},{27,19},{4,12},{13,5},{22,30},{31,23}} | collective-permute-start | bytes 3145736 | tf_op jit(solution)/shard_map/ppermute | solution.py:242
  886.4 37.2 %collective-permute-start.10 = (f32[4,256,256]{2,1,0:T(8,128)S(1)}, f32[4,256,256]{2,1,0:T(8,128)S(1)}, u32[]{:S(2)}, u32[]{:S(2)}) collective-permute-start(f32[4,256,256]{2,1,0:T(8,128)S(1)} %get-tuple-element.35), channel_id=1, source_target_pairs={{0,16},{9,25},{18,2},{27,11},{4,20},{13,29},{22,6},{31,15}} | collective-permute-start | bytes 3145736 | tf_op jit(solution)/shard_map/ppermute | solution.py:242
  887.9 62.4 %collective-permute-start.5 = (f32[4,256,256]{2,1,0:T(8,128)S(1)}, f32[4,256,256]{2,1,0:T(8,128)S(1)}, u32[]{:S(2)}, u32[]{:S(2)}) collective-permute-start(f32[4,256,256]{2,1,0:T(8,128)S(1)} %broadcast_select_fusion.10), channel_id=1, source_target_pairs={{0,16},{8,24},{9,25},{1,17},{18,2},{26,10},{27,11},{19,3},{4,20},{... | collective-permute-start | bytes 3145736 | tf_op jit(solution)/shard_map/ppermute | solution.py:242
  889.4 61.0 %collective-permute-start.7 = (f32[4,256,256]{2,1,0:T(8,128)S(1)}, f32[4,256,256]{2,1,0:T(8,128)S(1)}, u32[]{:S(2)}, u32[]{:S(2)}) collective-permute-start(f32[4,256,256]{2,1,0:T(8,128)S(1)} %broadcast_select_fusion.4), channel_id=1, source_target_pairs={{0,8},{16,24},{9,1},{25,17},{18,26},{2,10},{27,19},{11,3},{4,12},{... | collective-permute-start | bytes 3145736 | tf_op jit(solution)/shard_map/ppermute | solution.py:242
  907.1 63.1 %collective-permute-start.9 = (f32[4,256,256]{2,1,0:T(8,128)S(1)}, f32[4,256,256]{2,1,0:T(8,128)S(1)}, u32[]{:S(2)}, u32[]{:S(2)}) collective-permute-start(f32[4,256,256]{2,1,0:T(8,128)S(1)} %broadcast_select_fusion.9), channel_id=1, source_target_pairs={{0,16},{8,24},{9,25},{1,17},{18,2},{26,10},{27,11},{19,3},{4,20},{... | collective-permute-start | bytes 3145736 | tf_op jit(solution)/shard_map/ppermute | solution.py:242
  923.8 46.6 %collective-permute-start.11 = (f32[4,256,256]{2,1,0:T(8,128)S(1)}, f32[4,256,256]{2,1,0:T(8,128)S(1)}, u32[]{:S(2)}, u32[]{:S(2)}) collective-permute-start(f32[4,256,256]{2,1,0:T(8,128)S(1)} %broadcast_select_fusion.3), channel_id=1, source_target_pairs={{0,8},{16,24},{9,1},{25,17},{18,26},{2,10},{27,19},{11,3},{4,12},{... | collective-permute-start | bytes 3145736 | tf_op jit(solution)/shard_map/ppermute | solution.py:242
  972.1 113.0 %copy-start.1 = (s32[8]{0:T(128)S(1)}, s32[8]{0:T(128)}, u32[]{:S(2)}) copy-start(s32[8]{0:T(128)} %param.9) | copy-start | bytes 100
  (6 other events, 23.7 us)
Sparse Core Ops, SparseCore 0:
  448.2 233.7 all-reduce.4
  684.5 96.0 all-reduce.6
  783.1 97.7 all-reduce.10
  883.9 79.7 all-reduce.8
